TPU v7x, 128 devices: a whole 4x4x4 slice. The times are simulated.
128 devices in a mesh: dp: 8 (over z_hi, x), tensor: 16 (over y, z_lo, core).
Axes of the slice: x: 4, y: 4, z: 4 (z_hi: 2, z_lo: 2; z = z_hi * 2 + z_lo), core: 2. Of those that a mesh axis runs over, the one named last changes fastest.
Arguments:
- inputs: bfloat16 [16, 1024, 2048], P('dp', 'tensor'), may hold values from -6 to 6
- teacher: bfloat16 [16, 1024, 2048], P('dp', 'tensor'), may hold values from -6 to 6
- segment_ids: int32 [16, 1024], P('dp'), may hold values from 0 to 3, never falling along the last dimension, each value on 1 to 512 neighbouring positions
- padding: int32 [16, 1024], P('dp', 'tensor'), may hold values from 0 to 1, as said below
- attn_gain: float32 [2048], replicated, may hold values from 0.5 to 1.5
- qkv_weight: bfloat16 [2048, 3, 2048], P('dp', None, 'tensor'), may hold values from -0.125 to 0.125
- beta_weight: bfloat16 [2048, 16], P('dp', 'tensor'), may hold values from -0.125 to 0.125
- conv_taps: bfloat16 [4, 3, 16, 128], P(None, None, 'tensor', 'dp'), may hold values from -4 to 4
- head_gain: bfloat16 [16, 128], P('tensor', 'dp'), may hold values from 0.5 to 1.5
- out_weight: bfloat16 [2048, 2048], P('tensor', 'dp'), may hold values from -0.125 to 0.125
- mlp_gain: float32 [2048], replicated, may hold values from 0.5 to 1.5
- gate_weight: bfloat16 [2048, 5632], P('dp', 'tensor'), may hold values from -0.125 to 0.125
- up_weight: bfloat16 [2048, 5632], P('dp', 'tensor'), may hold values from -0.125 to 0.125
- down_weight: bfloat16 [5632, 2048], P('tensor', 'dp'), may hold values from -0.15625 to 0.15625
Outputs:
- block_out: bfloat16 [16, 1024, 2048], P('dp', 'tensor')
- loss: float32 [], replicated
- input_grad: float32 [16, 1024, 2048], P('dp', 'tensor')
- attn_gain_grad: float32 [2048], replicated
- qkv_grad: float32 [2048, 3, 2048], P('dp', None, 'tensor')
- beta_grad: float32 [2048, 16], P('dp', 'tensor')
- taps_grad: float32 [4, 3, 16, 128], P(None, None, 'tensor', 'dp')
- head_gain_grad: float32 [16, 128], P('tensor', 'dp')
- out_grad: float32 [2048, 2048], P('tensor', 'dp')
- mlp_gain_grad: float32 [2048], replicated
- gate_grad: float32 [2048, 5632], P('dp', 'tensor')
- up_grad: float32 [2048, 5632], P('dp', 'tensor')
- down_grad: float32 [5632, 2048], P('tensor', 'dp')
Inputs may be any that keep to these rules, and one draw needn't show every extreme that they name: `padding`: in each sequence the tokens that count form a leading run of 256 to 767 tokens; the rest are 0. `segment_ids`: document numbers never fall along a sequence; a document has 1 to 512 tokens.
All inputs are finite; a program needn't handle non-finite values.
Results may differ from a plain program's by a relative error of at most 0.029.
Values may be sent and summed in bfloat16 or wider, within the bound.
A program may use at most 192 MiB of HBM per device.

v0:
```python
import jax
import jax.numpy as jnp
from jax import lax
from jax.sharding import PartitionSpec as P

GROUP = 64
highest = lax.Precision.HIGHEST


def rms_norm(values, epsilon):
    return values * lax.rsqrt(jnp.mean(values * values, -1, keepdims=True) + epsilon)


def unit_norm(values):
    return values * lax.rsqrt(jnp.sum(values * values, -1, keepdims=True) + 1e-06)


def short_conv(fields, taps, segment):
    length = fields.shape[0]
    total = fields * taps[0]
    for offset in range(1, taps.shape[0]):
        blank_rows = jnp.zeros((offset,) + fields.shape[1:], fields.dtype)
        moved = jnp.concatenate([blank_rows, fields[: length - offset]], 0)
        earlier = jnp.concatenate(
            [jnp.full((offset,), -1, jnp.int32), segment[: length - offset]], 0
        )
        keep = (earlier == segment).astype(fields.dtype)
        total = total + moved * keep[:, None, None, None] * taps[offset]
    return total


def delta_block(carry, block):
    state, previous = carry
    query, keys, values, beta, segment = block
    size = segment.shape[0]
    dtype = state.dtype
    carried = (segment == previous).astype(dtype)
    same = (segment[:, None] == segment[None, :]).astype(dtype)
    strict = jnp.tril(jnp.ones((size, size), dtype), -1)
    within = jnp.tril(jnp.ones((size, size), dtype))
    gram = jnp.einsum("htk,hsk->hts", keys, keys, precision=highest)
    mixing = gram * beta[:, None, :] * (same * strict)
    recalled = jnp.einsum("htk,hvk->htv", keys, state, precision=highest)
    target = values - carried[None, :, None] * recalled
    system = jnp.eye(size, dtype=dtype)[None] + mixing
    updates = jax.vmap(
        lambda matrix, right: jax.scipy.linalg.solve_triangular(
            matrix, right, lower=True, unit_diagonal=True
        )
    )(system, target)
    weighted = updates * beta[:, :, None]
    scores = jnp.einsum("htk,hsk->hts", query, keys, precision=highest) * (same * within)
    output = carried[None, :, None] * jnp.einsum("htk,hvk->htv", query, state, precision=highest)
    output = output + jnp.einsum("hts,hsv->htv", scores, weighted, precision=highest)
    closing = (segment == segment[size - 1]).astype(dtype)
    new_state = carried[size - 1] * state + jnp.einsum(
        "hsv,hsk->hvk", weighted * closing[None, :, None], keys, precision=highest
    )
    return ((new_state, segment[size - 1]), output)


def mixer(projected, beta_logit, taps, head_gain, segment):
    length = projected.shape[0]
    heads = beta_logit.shape[1]
    width = taps.shape[-1]
    fields = projected.reshape(length, 3, heads, width)
    mixed = jax.nn.silu(short_conv(fields, taps, segment))
    query = unit_norm(mixed[:, 0]) * width ** (-0.5)
    keys = unit_norm(mixed[:, 1])
    values = mixed[:, 2]
    beta = jax.nn.sigmoid(beta_logit)
    blocks = length // GROUP

    def arrange(array):
        return jnp.transpose(array.reshape(blocks, GROUP, heads, width), (0, 2, 1, 3))

    beta_blocks = jnp.transpose(beta.reshape(blocks, GROUP, heads), (0, 2, 1))
    segment_blocks = segment.reshape(blocks, GROUP)
    start = (jnp.zeros((heads, width, width), projected.dtype), jnp.int32(-1))
    final, outputs = lax.scan(
        jax.checkpoint(delta_block),
        start,
        (arrange(query), arrange(keys), arrange(values), beta_blocks, segment_blocks),
    )
    raw = jnp.transpose(outputs, (0, 2, 1, 3)).reshape(length, heads, width)
    normed = rms_norm(raw, 1e-05) * head_gain
    return normed.reshape(length, heads * width)


def fetch(
    qkv_weight, beta_weight, conv_taps, head_gain, out_weight, gate_weight, up_weight, down_weight
):
    return (
        lax.all_gather(qkv_weight, "dp", axis=0, tiled=True),
        lax.all_gather(beta_weight, "dp", axis=0, tiled=True),
        lax.all_gather(conv_taps, "dp", axis=3, tiled=True),
        lax.all_gather(head_gain, "dp", axis=1, tiled=True),
        lax.all_gather(out_weight, "dp", axis=1, tiled=True),
        lax.all_gather(gate_weight, "dp", axis=0, tiled=True),
        lax.all_gather(up_weight, "dp", axis=0, tiled=True),
        lax.all_gather(down_weight, "dp", axis=1, tiled=True),
    )


def settle(qkv_part, beta_part, taps_part, gain_part, out_part, gate_part, up_part, down_part):
    return (
        lax.psum_scatter(
            qkv_part.astype(jnp.bfloat16), "dp", scatter_dimension=0, tiled=True
        ).astype(jnp.float32),
        lax.psum_scatter(
            beta_part.astype(jnp.bfloat16), "dp", scatter_dimension=0, tiled=True
        ).astype(jnp.float32),
        lax.psum_scatter(
            taps_part.astype(jnp.bfloat16), "dp", scatter_dimension=3, tiled=True
        ).astype(jnp.float32),
        lax.psum_scatter(
            gain_part.astype(jnp.bfloat16), "dp", scatter_dimension=1, tiled=True
        ).astype(jnp.float32),
        lax.psum_scatter(
            out_part.astype(jnp.bfloat16), "dp", scatter_dimension=1, tiled=True
        ).astype(jnp.float32),
        lax.psum_scatter(
            gate_part.astype(jnp.bfloat16), "dp", scatter_dimension=0, tiled=True
        ).astype(jnp.float32),
        lax.psum_scatter(
            up_part.astype(jnp.bfloat16), "dp", scatter_dimension=0, tiled=True
        ).astype(jnp.float32),
        lax.psum_scatter(
            down_part.astype(jnp.bfloat16), "dp", scatter_dimension=1, tiled=True
        ).astype(jnp.float32),
    )


def widened(array, dim, factor):
    shape = list(array.shape)
    shape[dim] = shape[dim] * factor
    return jnp.zeros(tuple(shape), jnp.float32)


def body(
    inputs,
    teacher,
    segment_ids,
    padding,
    attn_gain,
    qkv_weight,
    beta_weight,
    conv_taps,
    head_gain,
    out_weight,
    mlp_gain,
    gate_weight,
    up_weight,
    down_weight,
):
    length = segment_ids.shape[1]
    dp_count = lax.axis_size("dp")
    all_rows = inputs.shape[0] * length * dp_count
    valid = lax.psum(jnp.sum(padding), ("dp", "tensor"))
    scale = all_rows / valid.astype(jnp.float32)
    shards = (
        qkv_weight,
        beta_weight,
        conv_taps,
        head_gain,
        out_weight,
        gate_weight,
        up_weight,
        down_weight,
    )
    gather_dims = (0, 0, 3, 1, 1, 0, 0, 1)
    totals = tuple((widened(weight, dim, dp_count) for weight, dim in zip(shards, gather_dims)))
    zero_gain = jnp.zeros(attn_gain.shape, jnp.float32)

    def micro_step(carry, batch):
        totals, squares, attn_sum, mlp_sum = carry
        tokens, target, segment, mask = batch
        weights_now = fetch(
            qkv_weight,
            beta_weight,
            conv_taps,
            head_gain,
            out_weight,
            gate_weight,
            up_weight,
            down_weight,
        )
        qkv_full, beta_full, taps_full, gain_full, out_full, gate_full, up_full, down_full = (
            weights_now
        )
        tokens32 = tokens.astype(jnp.float32)
        attn_scale = lax.rsqrt(jnp.mean(tokens32 * tokens32, -1, keepdims=True) + 1e-06)
        attn_unit = tokens32 * attn_scale
        normed = (attn_unit * attn_gain).astype(jnp.bfloat16)
        gathered = lax.all_gather(normed, "tensor", axis=0, tiled=True)
        projected = jnp.einsum(
            "sd,dcf->scf", gathered, qkv_full, preferred_element_type=jnp.float32
        )
        beta_logit = jnp.dot(gathered, beta_full, preferred_element_type=jnp.float32)

        def local_mixer(projected_in, beta_in, taps_in, gain_in):
            return mixer(projected_in, beta_in, taps_in, gain_in, segment)

        heads_out, mixer_back = jax.vjp(
            local_mixer,
            projected,
            beta_logit,
            taps_full.astype(jnp.float32),
            gain_full.astype(jnp.float32),
        )
        heads_low = heads_out.astype(jnp.bfloat16)
        attention = lax.psum_scatter(
            jnp.dot(heads_low, out_full, preferred_element_type=jnp.float32).astype(jnp.bfloat16),
            "tensor",
            scatter_dimension=0,
            tiled=True,
        ).astype(jnp.float32)
        hidden = tokens32 + attention
        mlp_scale = lax.rsqrt(jnp.mean(hidden * hidden, -1, keepdims=True) + 1e-06)
        mlp_unit = hidden * mlp_scale
        ffn_in = (mlp_unit * mlp_gain).astype(jnp.bfloat16)
        ffn_all = lax.all_gather(ffn_in, "tensor", axis=0, tiled=True)
        gate = jnp.dot(ffn_all, gate_full, preferred_element_type=jnp.float32)
        up = jnp.dot(ffn_all, up_full, preferred_element_type=jnp.float32)
        sigma = jax.nn.sigmoid(gate)
        act = (gate * sigma * up).astype(jnp.bfloat16)
        output = hidden + lax.psum_scatter(
            jnp.dot(act, down_full, preferred_element_type=jnp.float32).astype(jnp.bfloat16),
            "tensor",
            scatter_dimension=0,
            tiled=True,
        ).astype(jnp.float32)
        diff = output - target.astype(jnp.float32)
        mask32 = mask.astype(jnp.float32)
        squares = squares + jnp.sum(jnp.sum(diff * diff, -1) * mask32)
        block_grad = (scale * mask32)[:, None] * diff
        weights_back = fetch(
            qkv_weight,
            beta_weight,
            conv_taps,
            head_gain,
            out_weight,
            gate_weight,
            up_weight,
            down_weight,
        )
        qkv_back, beta_back, taps_back, gain_back, out_back, gate_back, up_back, down_back = (
            weights_back
        )
        ffn_grad_all = lax.all_gather(block_grad.astype(jnp.bfloat16), "tensor", axis=0, tiled=True)
        down_part = jnp.einsum("sf,sd->fd", act, ffn_grad_all, preferred_element_type=jnp.float32)
        act_grad = jnp.einsum(
            "sd,fd->sf", ffn_grad_all, down_back, preferred_element_type=jnp.float32
        )
        gate_low = (act_grad * up * sigma * (1.0 + gate * (1.0 - sigma))).astype(jnp.bfloat16)
        up_low = (act_grad * gate * sigma).astype(jnp.bfloat16)
        gate_part = jnp.einsum("sd,sf->df", ffn_all, gate_low, preferred_element_type=jnp.float32)
        up_part = jnp.einsum("sd,sf->df", ffn_all, up_low, preferred_element_type=jnp.float32)
        total = jnp.einsum("sf,df->sd", gate_low, gate_back, preferred_element_type=jnp.float32)
        mlp_grad = lax.psum_scatter(
            (
                total + jnp.einsum("sf,df->sd", up_low, up_back, preferred_element_type=jnp.float32)
            ).astype(jnp.bfloat16),
            "tensor",
            scatter_dimension=0,
            tiled=True,
        ).astype(jnp.float32)
        mlp_sum = mlp_sum + jnp.sum(mlp_grad * mlp_unit, 0)
        mlp_inner = mlp_grad * mlp_gain
        hidden_grad = block_grad + mlp_scale * (
            mlp_inner - mlp_unit * jnp.mean(mlp_inner * mlp_unit, -1, keepdims=True)
        )
        attention_all = lax.all_gather(
            hidden_grad.astype(jnp.bfloat16), "tensor", axis=0, tiled=True
        )
        out_part = jnp.einsum(
            "sf,sd->fd", heads_low, attention_all, preferred_element_type=jnp.float32
        )
        heads_grad = jnp.einsum(
            "sd,fd->sf", attention_all, out_back, preferred_element_type=jnp.float32
        )
        projected_grad, beta_logit_grad, taps_part, gain_part = mixer_back(heads_grad)
        projected_low = projected_grad.astype(jnp.bfloat16)
        beta_low = beta_logit_grad.astype(jnp.bfloat16)
        qkv_part = jnp.einsum(
            "sd,scf->dcf", gathered, projected_low, preferred_element_type=jnp.float32
        )
        beta_part = jnp.einsum("sd,sh->dh", gathered, beta_low, preferred_element_type=jnp.float32)
        total = jnp.einsum(
            "scf,dcf->sd", projected_low, qkv_back, preferred_element_type=jnp.float32
        )
        normed_grad = lax.psum_scatter(
            (
                total
                + jnp.einsum("sh,dh->sd", beta_low, beta_back, preferred_element_type=jnp.float32)
            ).astype(jnp.bfloat16),
            "tensor",
            scatter_dimension=0,
            tiled=True,
        ).astype(jnp.float32)
        attn_sum = attn_sum + jnp.sum(normed_grad * attn_unit, 0)
        attn_inner = normed_grad * attn_gain
        input_grad = hidden_grad + attn_scale * (
            attn_inner - attn_unit * jnp.mean(attn_inner * attn_unit, -1, keepdims=True)
        )
        parts = (qkv_part, beta_part, taps_part, gain_part, out_part, gate_part, up_part, down_part)
        totals = tuple((old + new for old, new in zip(totals, parts)))
        return ((totals, squares, attn_sum, mlp_sum), (output.astype(jnp.bfloat16), input_grad))

    start = (totals, jnp.zeros((), jnp.float32), zero_gain, zero_gain)
    finals, outputs = lax.scan(micro_step, start, (inputs, teacher, segment_ids, padding))
    totals, squares, attn_sum, mlp_sum = finals
    block_out, input_grad = outputs
    totals = settle(
        totals[0], totals[1], totals[2], totals[3], totals[4], totals[5], totals[6], totals[7]
    )
    attn_total, mlp_total, square_total = lax.psum((attn_sum, mlp_sum, squares), ("dp", "tensor"))
    loss = square_total / (valid.astype(jnp.float32) * inputs.shape[2])
    return (
        block_out,
        loss,
        input_grad,
        attn_total,
        totals[0],
        totals[1],
        totals[2],
        totals[3],
        totals[4],
        mlp_total,
        totals[5],
        totals[6],
        totals[7],
    )


def solution(mesh):
    in_specs = (
        P("dp", "tensor", None),
        P("dp", "tensor", None),
        P("dp", None),
        P("dp", "tensor"),
        P(),
        P("dp", None, "tensor"),
        P("dp", "tensor"),
        P(None, None, "tensor", "dp"),
        P("tensor", "dp"),
        P("tensor", "dp"),
        P(),
        P("dp", "tensor"),
        P("dp", "tensor"),
        P("tensor", "dp"),
    )
    out_specs = (
        P("dp", "tensor", None),
        P(),
        P("dp", "tensor", None),
        P(),
        P("dp", None, "tensor"),
        P("dp", "tensor"),
        P(None, None, "tensor", "dp"),
        P("tensor", "dp"),
        P("tensor", "dp"),
        P(),
        P("dp", "tensor"),
        P("dp", "tensor"),
        P("tensor", "dp"),
    )
    return jax.shard_map(body, mesh=mesh, in_specs=in_specs, out_specs=out_specs, check_vma=False)
```

profile of v0, /device:TPU:0, one launch (start us, length us, event | category | flops | bytes accessed | tf_op | source)
XLA Modules:
  0.0 3572.0 jit_solution(11940812805327868886)
XLA Ops:
  9.4 68.2 %psum.28 = s32[]{:T(128)} all-reduce(s32[]{:T(128)} %reduce_sum.286), channel_id=1, replica_groups=mesh['dp'=8,'tensor'=16] {'dp','tensor'}, use_global_device_ids=true, to_apply=%region_1.0 | all-reduce | flops 1 | bytes 8 | tf_op jit(solution)/shard_map/psum | solution.py:159
  79.7 2898.0 %while.135 = (s32[]{:T(128)}, f32[2048,3,128]{2,0,1:T(8,128)}, f32[2048,1]{0,1:T(1,128)}, f32[4,3,1,128]{3,2,1,0:T(1,128)}, f32[1,128]{1,0:T(1,128)}, /*index=5*...) while((s32[]{:T(128)}, f32[2048,3,128]{2,0,1:T(8,128)}, ...), condition=%wide.region_32.34_spmd.clone, body=%wide.region_2.33_spmd.clone.sunk | while | flops 20024219648 | bytes 558299264 | solution.py:311
  220.5 276.7 %while.136 = (s32[]{:T(128)}, f32[1,128,128]{2,1,0:T(8,128)S(1)}, s32[]{:T(128)}, f32[16,1,64,128]{3,2,1,0:T(8,128)}, f32[16,1,128,128]{3,2,1,0:T(8,128)}, /*ind...) while((s32[]{:T(128)}, f32[1,128,128]{2,1,0:T(8,128)S(1)}, ...), condition=%wide.region_7.8_spmd.clone, body=%wide.region_6.7_spmd.clone.sunk | while | flops 63140160 | bytes 960217 | solution.py:80
  505.5 63.9 %reduce-scatter.35.cloned.1.call-done = bf16[64,2048]{1,0:T(8,128)(2,1)} async-done(((bf16[1024,2048]{1,0:T(8,128)(2,1)}), bf16[64,2048]{1,0:T(8,128)(2,1)}) %reduce-scatter.35.cloned.1.call-update) | async-done | bytes 262160 | tf_op jit(solution)/shard_map/while/body/eval_jaxpr/reduce_scatter | solution.py:212
  574.1 47.6 %all-gather.15.cloned.1.call-done = bf16[2048,352]{0,1:T(8,128)(2,1)} async-done(((bf16[256,352]{0,1:T(8,128)(2,1)}), bf16[2048,352]{0,1:T(8,128)(2,1)}) %all-gather.15.cloned.1.call-update) | async-done | bytes 1441808 | tf_op jit(solution)/shard_map/while/body/eval_jaxpr/all_gather | solution.py:99
  665.5 48.5 %all-gather.17.cloned.1.call-done = bf16[2048,352]{0,1:T(8,128)(2,1)} async-done(((bf16[256,352]{0,1:T(8,128)(2,1)}), bf16[2048,352]{0,1:T(8,128)(2,1)}) %all-gather.17.cloned.1.call-update) | async-done | bytes 1441808 | tf_op jit(solution)/shard_map/while/body/eval_jaxpr/all_gather | solution.py:100
  720.2 46.5 %all-gather.19.cloned.1.call-done = bf16[352,2048]{1,0:T(8,128)(2,1)} async-done(((bf16[352,256]{1,0:T(8,128)(2,1)}), bf16[352,2048]{1,0:T(8,128)(2,1)}) %all-gather.19.cloned.1.call-update) | async-done | bytes 1441808 | tf_op jit(solution)/shard_map/while/body/eval_jaxpr/all_gather | solution.py:101
  773.4 65.7 %reduce-scatter.37.cloned.1.call-done = bf16[64,2048]{1,0:T(8,128)(2,1)} async-done(((bf16[1024,2048]{1,0:T(8,128)(2,1)}), bf16[64,2048]{1,0:T(8,128)(2,1)}) %reduce-scatter.37.cloned.1.call-update) | async-done | bytes 262160 | tf_op jit(solution)/shard_map/while/body/eval_jaxpr/reduce_scatter | solution.py:227
  890.6 67.3 %reduce-scatter.39.cloned.1.call-done = bf16[64,2048]{1,0:T(8,128)(2,1)} async-done(((bf16[1024,2048]{1,0:T(8,128)(2,1)}), bf16[64,2048]{1,0:T(8,128)(2,1)}) %reduce-scatter.39.cloned.1.call-update) | async-done | bytes 262160 | tf_op jit(solution)/shard_map/while/body/eval_jaxpr/reduce_scatter | solution.py:260
  1007.3 429.0 %while.137 = (s32[]{:T(128)}, f32[1,128,128]{2,1,0:T(8,128)S(1)}, f32[16,1,64,128]{3,2,1,0:T(8,128)}, f32[16,1,64,128]{3,2,1,0:T(8,128)}, f32[16,1,64,128]{3,2,1...) while((s32[]{:T(128)}, f32[1,128,128]{2,1,0:T(8,128)S(1)}, ...), condition=%wide.region_18.19_spmd.clone, body=%wide.region_15.18_spmd.clone.sunk | while | flops 160874752 | bytes 2876935 | solution.py:80
  1669.5 276.7 %while.136 = (s32[]{:T(128)}, f32[1,128,128]{2,1,0:T(8,128)S(1)}, s32[]{:T(128)}, f32[16,1,64,128]{3,2,1,0:T(8,128)}, f32[16,1,128,128]{3,2,1,0:T(8,128)}, /*ind...) while((s32[]{:T(128)}, f32[1,128,128]{2,1,0:T(8,128)S(1)}, ...), condition=%wide.region_7.8_spmd.clone, body=%wide.region_6.7_spmd.clone.sunk | while | flops 63140160 | bytes 960217 | solution.py:80
  1954.4 62.5 %reduce-scatter.35.cloned.1.call-done = bf16[64,2048]{1,0:T(8,128)(2,1)} async-done(((bf16[1024,2048]{1,0:T(8,128)(2,1)}), bf16[64,2048]{1,0:T(8,128)(2,1)}) %reduce-scatter.35.cloned.1.call-update) | async-done | bytes 262160 | tf_op jit(solution)/shard_map/while/body/eval_jaxpr/reduce_scatter | solution.py:212
  2021.8 47.5 %all-gather.15.cloned.1.call-done = bf16[2048,352]{0,1:T(8,128)(2,1)} async-done(((bf16[256,352]{0,1:T(8,128)(2,1)}), bf16[2048,352]{0,1:T(8,128)(2,1)}) %all-gather.15.cloned.1.call-update) | async-done | bytes 1441808 | tf_op jit(solution)/shard_map/while/body/eval_jaxpr/all_gather | solution.py:99
  2113.0 48.5 %all-gather.17.cloned.1.call-done = bf16[2048,352]{0,1:T(8,128)(2,1)} async-done(((bf16[256,352]{0,1:T(8,128)(2,1)}), bf16[2048,352]{0,1:T(8,128)(2,1)}) %all-gather.17.cloned.1.call-update) | async-done | bytes 1441808 | tf_op jit(solution)/shard_map/while/body/eval_jaxpr/all_gather | solution.py:100
  2220.9 65.7 %reduce-scatter.37.cloned.1.call-done = bf16[64,2048]{1,0:T(8,128)(2,1)} async-done(((bf16[1024,2048]{1,0:T(8,128)(2,1)}), bf16[64,2048]{1,0:T(8,128)(2,1)}) %reduce-scatter.37.cloned.1.call-update) | async-done | bytes 262160 | tf_op jit(solution)/shard_map/while/body/eval_jaxpr/reduce_scatter | solution.py:227
  2337.9 67.5 %reduce-scatter.39.cloned.1.call-done = bf16[64,2048]{1,0:T(8,128)(2,1)} async-done(((bf16[1024,2048]{1,0:T(8,128)(2,1)}), bf16[64,2048]{1,0:T(8,128)(2,1)}) %reduce-scatter.39.cloned.1.call-update) | async-done | bytes 262160 | tf_op jit(solution)/shard_map/while/body/eval_jaxpr/reduce_scatter | solution.py:260
  2455.1 429.0 %while.137 = (s32[]{:T(128)}, f32[1,128,128]{2,1,0:T(8,128)S(1)}, f32[16,1,64,128]{3,2,1,0:T(8,128)}, f32[16,1,64,128]{3,2,1,0:T(8,128)}, f32[16,1,64,128]{3,2,1...) while((s32[]{:T(128)}, f32[1,128,128]{2,1,0:T(8,128)S(1)}, ...), condition=%wide.region_18.19_spmd.clone, body=%wide.region_15.18_spmd.clone.sunk | while | flops 160874752 | bytes 2876935 | solution.py:80
  2997.1 66.0 %all-reduce.17 = (f32[]{:T(128)}, f32[2048]{0:T(1024)}, f32[2048]{0:T(1024)}) all-reduce(f32[]{:T(128)} %get-tuple-element.997, f32[2048]{0:T(1024)S(1)} %copy-done.68, f32[2048]{0:T(1024)S(1)} %copy-done.65), channel_id=1, replica_groups=mesh['dp'=8,'tensor'=16] {'dp','tensor'}, use_global_device_ids=true, to_apply=%region_33.35 | all-reduce | flops 4097 | bytes 32776 | tf_op jit(solution)/shard_map/psum | solution.py:317
  3110.2 71.8 %reduce-scatter.29.cloned.1.call-done = bf16[256,1]{1,0:T(8,128)(2,1)} async-done(((bf16[2048,1]{1,0:T(8,128)(2,1)}), bf16[256,1]{1,0:T(8,128)(2,1)}) %reduce-scatter.29.cloned.1.call-update) | async-done | bytes 528
  3183.5 72.5 %reduce-scatter.21.cloned.1.call-done = bf16[128,256]{1,0:T(8,128)(2,1)} async-done(((bf16[128,2048]{1,0:T(8,128)(2,1)}), bf16[128,256]{1,0:T(8,128)(2,1)}) %reduce-scatter.21.cloned.1.call-update) | async-done | bytes 65552 | tf_op jit(solution)/shard_map/reduce_scatter | solution.py:119
  3257.5 74.5 %reduce-scatter.23.cloned.1.call-done = bf16[256,352]{0,1:T(8,128)(2,1)} async-done(((bf16[2048,352]{0,1:T(8,128)(2,1)}), bf16[256,352]{0,1:T(8,128)(2,1)}) %reduce-scatter.23.cloned.1.call-update) | async-done | bytes 180240 | tf_op jit(solution)/shard_map/reduce_scatter | solution.py:122
  3333.7 74.7 %reduce-scatter.25.cloned.1.call-done = bf16[256,352]{0,1:T(8,128)(2,1)} async-done(((bf16[2048,352]{0,1:T(8,128)(2,1)}), bf16[256,352]{0,1:T(8,128)(2,1)}) %reduce-scatter.25.cloned.1.call-update) | async-done | bytes 180240 | tf_op jit(solution)/shard_map/reduce_scatter | solution.py:125
  3410.1 74.2 %reduce-scatter.27.cloned.1.call-done = bf16[352,256]{1,0:T(8,128)(2,1)} async-done(((bf16[352,2048]{1,0:T(8,128)(2,1)}), bf16[352,256]{1,0:T(8,128)(2,1)}) %reduce-scatter.27.cloned.1.call-update) | async-done | bytes 180240 | tf_op jit(solution)/shard_map/reduce_scatter | solution.py:128
  3486.0 75.3 %reduce-scatter.19.cloned.1.call-done = bf16[256,3,128]{2,0,1:T(8,128)(2,1)} async-done(((bf16[2048,3,128]{2,0,1:T(8,128)(2,1)}), bf16[256,3,128]{2,0,1:T(8,128)(2,1)}) %reduce-scatter.19.cloned.1.call-update) | async-done | bytes 196624 | tf_op jit(solution)/shard_map/reduce_scatter | solution.py:107
  (2304 shorter events, 2310.4 us)
Async XLA Ops:
  80.0 121.4 %all-gather.9.cloned.1.call-start = ((), (), s32[]{:S(2)}) async-start(), calls=%async_computation.20 | async-start | bytes 1769472 | tf_op jit(solution)/shard_map/while/body/eval_jaxpr/all_gather | solution.py:94
  80.7 120.7 %all-gather.11.cloned.1.call-start = ((), (), s32[]{:S(2)}) async-start(), calls=%async_computation.21 | async-start | bytes 4456448 | tf_op jit(solution)/shard_map/while/body/eval_jaxpr/all_gather | solution.py:195
  84.3 485.1 %reduce-scatter.35.cloned.1.call-start = ((), (), s32[]{:S(2)}) async-start(), calls=%async_computation.22 | async-start | bytes 4456448 | tf_op jit(solution)/shard_map/while/body/eval_jaxpr/reduce_scatter | solution.py:212
  504.9 116.9 %all-gather.15.cloned.1.call-start = ((), (), s32[]{:S(2)}) async-start(), calls=%async_computation.24 | async-start | bytes 1622016 | tf_op jit(solution)/shard_map/while/body/eval_jaxpr/all_gather | solution.py:99
  505.4 154.6 %all-gather.13.cloned.1.call-start = ((), (), s32[]{:S(2)}) async-start(), calls=%async_computation.23 | async-start | bytes 4456448 | tf_op jit(solution)/shard_map/while/body/eval_jaxpr/all_gather | solution.py:222
  572.5 141.5 %all-gather.17.cloned.1.call-start = ((), (), s32[]{:S(2)}) async-start(), calls=%async_computation.25 | async-start | bytes 1622016 | tf_op jit(solution)/shard_map/while/body/eval_jaxpr/all_gather | solution.py:100
  573.1 193.6 %all-gather.19.cloned.1.call-start = ((), (), s32[]{:S(2)}) async-start(), calls=%async_computation.26 | async-start | bytes 1622016 | tf_op jit(solution)/shard_map/while/body/eval_jaxpr/all_gather | solution.py:101
  573.8 265.3 %reduce-scatter.37.cloned.1.call-start = ((), (), s32[]{:S(2)}) async-start(), calls=%async_computation.27 | async-start | bytes 4456448 | tf_op jit(solution)/shard_map/while/body/eval_jaxpr/reduce_scatter | solution.py:227
  962.5 560.4 %reduce-scatter.41.cloned.1.call-start = ((), (), s32[]{:S(2)}) async-start(), calls=%async_computation.31 | async-start | bytes 4456448 | tf_op jit(solution)/shard_map/while/body/eval_jaxpr/reduce_scatter | solution.py:292
  1526.3 124.0 %all-gather.9.cloned.1.call-start = ((), (), s32[]{:S(2)}) async-start(), calls=%async_computation.20 | async-start | bytes 1769472 | tf_op jit(solution)/shard_map/while/body/eval_jaxpr/all_gather | solution.py:94
  1527.1 123.3 %all-gather.11.cloned.1.call-start = ((), (), s32[]{:S(2)}) async-start(), calls=%async_computation.21 | async-start | bytes 4456448 | tf_op jit(solution)/shard_map/while/body/eval_jaxpr/all_gather | solution.py:195
  1530.7 486.2 %reduce-scatter.35.cloned.1.call-start = ((), (), s32[]{:S(2)}) async-start(), calls=%async_computation.22 | async-start | bytes 4456448 | tf_op jit(solution)/shard_map/while/body/eval_jaxpr/reduce_scatter | solution.py:212
  1954.4 153.2 %all-gather.13.cloned.1.call-start = ((), (), s32[]{:S(2)}) async-start(), calls=%async_computation.23 | async-start | bytes 4456448 | tf_op jit(solution)/shard_map/while/body/eval_jaxpr/all_gather | solution.py:222
  2020.0 141.5 %all-gather.17.cloned.1.call-start = ((), (), s32[]{:S(2)}) async-start(), calls=%async_computation.25 | async-start | bytes 1622016 | tf_op jit(solution)/shard_map/while/body/eval_jaxpr/all_gather | solution.py:100
  2020.6 193.6 %all-gather.19.cloned.1.call-start = ((), (), s32[]{:S(2)}) async-start(), calls=%async_computation.26 | async-start | bytes 1622016 | tf_op jit(solution)/shard_map/while/body/eval_jaxpr/all_gather | solution.py:101
  2021.4 265.3 %reduce-scatter.37.cloned.1.call-start = ((), (), s32[]{:S(2)}) async-start(), calls=%async_computation.27 | async-start | bytes 4456448 | tf_op jit(solution)/shard_map/while/body/eval_jaxpr/reduce_scatter | solution.py:227
  2409.9 560.7 %reduce-scatter.41.cloned.1.call-start = ((), (), s32[]{:S(2)}) async-start(), calls=%async_computation.31 | async-start | bytes 4456448 | tf_op jit(solution)/shard_map/while/body/eval_jaxpr/reduce_scatter | solution.py:292
  2979.3 129.4 %reduce-scatter.31.cloned.1.call-start = ((), (), s32[]{:S(2)}) async-start(), calls=%async_computation.18 | async-start | bytes 36864
  2982.1 200.0 %reduce-scatter.29.cloned.1.call-start = ((), (), s32[]{:S(2)}) async-start(), calls=%async_computation.17 | async-start | bytes 589824
  2983.9 272.1 %reduce-scatter.21.cloned.1.call-start = ((), (), s32[]{:S(2)}) async-start(), calls=%async_computation.13 | async-start | bytes 589824 | tf_op jit(solution)/shard_map/reduce_scatter | solution.py:119
  2984.9 347.2 %reduce-scatter.23.cloned.1.call-start = ((), (), s32[]{:S(2)}) async-start(), calls=%async_computation.14 | async-start | bytes 1622016 | tf_op jit(solution)/shard_map/reduce_scatter | solution.py:122
  2988.1 420.3 %reduce-scatter.25.cloned.1.call-start = ((), (), s32[]{:S(2)}) async-start(), calls=%async_computation.15 | async-start | bytes 1622016 | tf_op jit(solution)/shard_map/reduce_scatter | solution.py:125
  2991.6 492.7 %reduce-scatter.27.cloned.1.call-start = ((), (), s32[]{:S(2)}) async-start(), calls=%async_computation.16 | async-start | bytes 1622016 | tf_op jit(solution)/shard_map/reduce_scatter | solution.py:128
  2993.0 568.2 %reduce-scatter.19.cloned.1.call-start = ((), (), s32[]{:S(2)}) async-start(), calls=%async_computation.12 | async-start | bytes 1769472 | tf_op jit(solution)/shard_map/reduce_scatter | solution.py:107
  (174 other events, 7654.0 us)
Sparse Core Ops, SparseCore 0:
  83.4 47.3 all-gather.8
  133.3 36.9 all-gather.10
  505.0 64.3 reduce-scatter.34
  571.6 50.0 all-gather.14
  624.0 36.0 all-gather.12
  662.4 51.6 all-gather.16
  716.4 50.2 all-gather.18
  772.9 66.1 reduce-scatter.36
  841.5 35.9 all-gather.20
  890.2 67.6 reduce-scatter.38
  962.6 35.8 all-gather.22
  1455.1 67.7 reduce-scatter.40
  1529.8 49.6 all-gather.8
  1581.8 36.8 all-gather.10
  1953.9 62.9 reduce-scatter.34
  2019.2 50.0 all-gather.14
  2071.5 36.0 all-gather.12
  2109.9 51.6 all-gather.16
  2163.9 50.2 all-gather.18
  2220.4 66.1 reduce-scatter.36
  2289.0 35.9 all-gather.20
  2337.8 67.5 reduce-scatter.38
  2410.0 36.1 all-gather.22
  2902.9 67.6 reduce-scatter.40
Sparse Core Ops, SparseCore 1:
  2982.1 60.9 reduce-scatter.32
  3047.2 61.4 reduce-scatter.30
  3112.1 69.9 reduce-scatter.28
  3186.1 69.9 reduce-scatter.20
  3259.8 72.2 reduce-scatter.22
  3336.3 72.1 reduce-scatter.24
  3412.0 72.2 reduce-scatter.26
  3488.4 72.8 reduce-scatter.18
where the time goes:
time: 3600 us; the launch traced here: 3570 us
  waiting for transfers between devices  1470 us (41%)
  other arithmetic  714 us (20%)
  matrix products  617 us (17%)
  blocking collectives  359 us (10%)
  local copies, waits for them, and re-layouts  359 us (10%)
    another operation x224, other arithmetic, delta_block(): jax.scipy.linalg.solve_triangular(matrix, right, lower=True, unit_diagona...  476 us
    reduce_scatter x2, waiting for transfers between devices, micro_step(): lax.psum_scatter((total + jnp.einsum('sf,df->sd', up_low, up_back, prefer...  135 us
    reduce_scatter x2, waiting for transfers between devices, micro_step(): lax.psum_scatter(jnp.dot(act, down_full, preferred_element_type=jnp.float...  131 us
    reduce_scatter x2, waiting for transfers between devices, micro_step(): lax.psum_scatter(jnp.dot(heads_low, out_full, preferred_element_type=jnp....  126 us
    squeeze x160, local copies, waits for them, and re-layouts, mixer(): lax.scan(jax.checkpoint(delta_block), start, (arrange(query), arrange(key...  119 us
    unnamed x11, waiting for transfers between devices  116 us
    dot_general x96, matrix products, delta_block(): jnp.einsum('hsv,hsk->hvk', weighted * closing[None, :, None], keys, preci...  108 us
    all_gather x2, waiting for transfers between devices, fetch(): lax.all_gather(up_weight, 'dp', axis=0, tiled=True)  97 us
  transfers between devices with their start and end apart: 32, of which 27 were waited for; matrix products, arithmetic and copies ran while one was open for 3% of the time, Pallas kernels for 0%

commit v1 on v0

--- a/solution.py
+++ b/solution.py
@@ -219,7 +219,12 @@
         mlp_scale = lax.rsqrt(jnp.mean(hidden * hidden, -1, keepdims=True) + 1e-06)
         mlp_unit = hidden * mlp_scale
         ffn_in = (mlp_unit * mlp_gain).astype(jnp.bfloat16)
-        ffn_all = lax.all_gather(ffn_in, "tensor", axis=0, tiled=True)
+        buffers = []
+        for _ in range(lax.axis_size("tensor")):
+            buffers.append(ffn_in)
+        main = jnp.stack(buffers, axis=0)
+        x_next = lax.all_to_all(main, "tensor", 0, 0)
+        ffn_all = jnp.concatenate(x_next, axis=0)
         gate = jnp.dot(ffn_all, gate_full, preferred_element_type=jnp.float32)
         up = jnp.dot(ffn_all, up_full, preferred_element_type=jnp.float32)
         sigma = jax.nn.sigmoid(gate)

time: 3600 us -> 3580 us (level)
  waiting for transfers between devices: 1470 us -> 1420 us
    all_gather x2 -> x0, waiting for transfers between devices: 76.7 us -> none  [micro_step(): ffn_all = lax.all_gather(ffn_in, 'tensor', axis=0, tiled=True)]
  transfers between devices with their start and end apart: 32 -> 32, of which waited for: 27 -> 25; matrix products, arithmetic and copies ran while one was open for 3% -> 4% of each run, Pallas kernels for 0% -> 0%
where the time goes in v1:
time: 3580 us; the launch traced here: 3560 us
  waiting for transfers between devices  1420 us (40%)
  other arithmetic  716 us (20%)
  matrix products  632 us (18%)
  local copies, waits for them, and re-layouts  366 us (10%)
  blocking collectives  359 us (10%)
    another operation x224, other arithmetic, delta_block(): jax.scipy.linalg.solve_triangular(matrix, right, lower=True, unit_diagona...  476 us
    reduce_scatter x2, waiting for transfers between devices, micro_step(): lax.psum_scatter((total + jnp.einsum('sf,df->sd', up_low, up_back, prefer...  135 us
    reduce_scatter x2, waiting for transfers between devices, micro_step(): lax.psum_scatter(jnp.dot(act, down_full, preferred_element_type=jnp.float...  131 us
    reduce_scatter x2, waiting for transfers between devices, micro_step(): lax.psum_scatter(jnp.dot(heads_low, out_full, preferred_element_type=jnp....  126 us
    all_gather x2, waiting for transfers between devices, fetch(): lax.all_gather(gate_weight, 'dp', axis=0, tiled=True)  124 us
    squeeze x160, local copies, waits for them, and re-layouts, mixer(): lax.scan(jax.checkpoint(delta_block), start, (arrange(query), arrange(key...  120 us
    unnamed x11, waiting for transfers between devices  116 us
    dot_general x96, matrix products, delta_block(): jnp.einsum('hsv,hsk->hvk', weighted * closing[None, :, None], keys, preci...  111 us
  transfers between devices with their start and end apart: 32, of which 25 were waited for; matrix products, arithmetic and copies ran while one was open for 4% of the time, Pallas kernels for 0%

profile of v1, /device:TPU:0, one launch (start us, length us, event | category | flops | bytes accessed | tf_op | source)
XLA Modules:
  0.0 3557.5 jit_solution(8500744530600312004)
XLA Ops:
  9.4 68.2 %psum.28 = s32[]{:T(128)} all-reduce(s32[]{:T(128)} %reduce_sum.286), channel_id=1, replica_groups=mesh['dp'=8,'tensor'=16] {'dp','tensor'}, use_global_device_ids=true, to_apply=%region_1.0 | all-reduce | flops 1 | bytes 8 | tf_op jit(solution)/shard_map/psum | solution.py:159
  79.7 2883.3 %while.135 = (s32[]{:T(128)}, f32[2048,3,128]{2,0,1:T(8,128)}, f32[2048,1]{0,1:T(1,128)}, f32[4,3,1,128]{3,2,1,0:T(1,128)}, f32[1,128]{1,0:T(1,128)}, /*index=5*...) while((s32[]{:T(128)}, f32[2048,3,128]{2,0,1:T(8,128)}, ...), condition=%wide.region_32.34_spmd.clone, body=%wide.region_2.33_spmd.clone.sunk | while | flops 20024219648 | bytes 537590272 | solution.py:316
  220.6 277.8 %while.136 = (s32[]{:T(128)}, f32[1,128,128]{2,1,0:T(8,128)S(1)}, s32[]{:T(128)}, f32[16,1,64,128]{3,2,1,0:T(8,128)}, f32[16,1,128,128]{3,2,1,0:T(8,128)}, /*ind...) while((s32[]{:T(128)}, f32[1,128,128]{2,1,0:T(8,128)S(1)}, ...), condition=%wide.region_7.8_spmd.clone, body=%wide.region_6.7_spmd.clone.sunk | while | flops 63140160 | bytes 960217 | solution.py:80
  506.5 63.7 %reduce-scatter.35.cloned.1.call-done = bf16[64,2048]{1,0:T(8,128)(2,1)} async-done(((bf16[1024,2048]{1,0:T(8,128)(2,1)}), bf16[64,2048]{1,0:T(8,128)(2,1)}) %reduce-scatter.35.cloned.1.call-update) | async-done | bytes 262160 | tf_op jit(solution)/shard_map/while/body/eval_jaxpr/reduce_scatter | solution.py:212
  581.3 62.0 %all-gather.12.cloned.1.call-done = bf16[2048,352]{0,1:T(8,128)(2,1)} async-done(((bf16[256,352]{0,1:T(8,128)(2,1)}), bf16[2048,352]{0,1:T(8,128)(2,1)}) %all-gather.12.cloned.1.call-update) | async-done | bytes 1441808 | tf_op jit(solution)/shard_map/while/body/eval_jaxpr/all_gather | solution.py:99
  648.8 52.7 %all-gather.14.cloned.1.call-done = bf16[2048,352]{0,1:T(8,128)(2,1)} async-done(((bf16[256,352]{0,1:T(8,128)(2,1)}), bf16[2048,352]{0,1:T(8,128)(2,1)}) %all-gather.14.cloned.1.call-update) | async-done | bytes 1441808 | tf_op jit(solution)/shard_map/while/body/eval_jaxpr/all_gather | solution.py:100
  707.7 46.4 %all-gather.16.cloned.1.call-done = bf16[352,2048]{1,0:T(8,128)(2,1)} async-done(((bf16[352,256]{1,0:T(8,128)(2,1)}), bf16[352,2048]{1,0:T(8,128)(2,1)}) %all-gather.16.cloned.1.call-update) | async-done | bytes 1441808 | tf_op jit(solution)/shard_map/while/body/eval_jaxpr/all_gather | solution.py:101
  760.8 65.7 %reduce-scatter.37.cloned.1.call-done = bf16[64,2048]{1,0:T(8,128)(2,1)} async-done(((bf16[1024,2048]{1,0:T(8,128)(2,1)}), bf16[64,2048]{1,0:T(8,128)(2,1)}) %reduce-scatter.37.cloned.1.call-update) | async-done | bytes 262160 | tf_op jit(solution)/shard_map/while/body/eval_jaxpr/reduce_scatter | solution.py:232
  878.0 67.2 %reduce-scatter.39.cloned.1.call-done = bf16[64,2048]{1,0:T(8,128)(2,1)} async-done(((bf16[1024,2048]{1,0:T(8,128)(2,1)}), bf16[64,2048]{1,0:T(8,128)(2,1)}) %reduce-scatter.39.cloned.1.call-update) | async-done | bytes 262160 | tf_op jit(solution)/shard_map/while/body/eval_jaxpr/reduce_scatter | solution.py:265
  994.8 434.5 %while.137 = (s32[]{:T(128)}, f32[1,128,128]{2,1,0:T(8,128)S(1)}, f32[16,1,64,128]{3,2,1,0:T(8,128)}, f32[16,1,64,128]{3,2,1,0:T(8,128)}, f32[16,1,64,128]{3,2,1...) while((s32[]{:T(128)}, f32[1,128,128]{2,1,0:T(8,128)S(1)}, ...), condition=%wide.region_18.19_spmd.clone, body=%wide.region_15.18_spmd.clone.sunk | while | flops 160874752 | bytes 2876935 | solution.py:80
  1662.2 277.7 %while.136 = (s32[]{:T(128)}, f32[1,128,128]{2,1,0:T(8,128)S(1)}, s32[]{:T(128)}, f32[16,1,64,128]{3,2,1,0:T(8,128)}, f32[16,1,128,128]{3,2,1,0:T(8,128)}, /*ind...) while((s32[]{:T(128)}, f32[1,128,128]{2,1,0:T(8,128)S(1)}, ...), condition=%wide.region_7.8_spmd.clone, body=%wide.region_6.7_spmd.clone.sunk | while | flops 63140160 | bytes 960217 | solution.py:80
  1948.2 62.5 %reduce-scatter.35.cloned.1.call-done = bf16[64,2048]{1,0:T(8,128)(2,1)} async-done(((bf16[1024,2048]{1,0:T(8,128)(2,1)}), bf16[64,2048]{1,0:T(8,128)(2,1)}) %reduce-scatter.35.cloned.1.call-update) | async-done | bytes 262160 | tf_op jit(solution)/shard_map/while/body/eval_jaxpr/reduce_scatter | solution.py:212
  2021.9 61.7 %all-gather.12.cloned.1.call-done = bf16[2048,352]{0,1:T(8,128)(2,1)} async-done(((bf16[256,352]{0,1:T(8,128)(2,1)}), bf16[2048,352]{0,1:T(8,128)(2,1)}) %all-gather.12.cloned.1.call-update) | async-done | bytes 1441808 | tf_op jit(solution)/shard_map/while/body/eval_jaxpr/all_gather | solution.py:99
  2089.0 52.8 %all-gather.14.cloned.1.call-done = bf16[2048,352]{0,1:T(8,128)(2,1)} async-done(((bf16[256,352]{0,1:T(8,128)(2,1)}), bf16[2048,352]{0,1:T(8,128)(2,1)}) %all-gather.14.cloned.1.call-update) | async-done | bytes 1441808 | tf_op jit(solution)/shard_map/while/body/eval_jaxpr/all_gather | solution.py:100
  2201.1 65.7 %reduce-scatter.37.cloned.1.call-done = bf16[64,2048]{1,0:T(8,128)(2,1)} async-done(((bf16[1024,2048]{1,0:T(8,128)(2,1)}), bf16[64,2048]{1,0:T(8,128)(2,1)}) %reduce-scatter.37.cloned.1.call-update) | async-done | bytes 262160 | tf_op jit(solution)/shard_map/while/body/eval_jaxpr/reduce_scatter | solution.py:232
  2317.9 67.5 %reduce-scatter.39.cloned.1.call-done = bf16[64,2048]{1,0:T(8,128)(2,1)} async-done(((bf16[1024,2048]{1,0:T(8,128)(2,1)}), bf16[64,2048]{1,0:T(8,128)(2,1)}) %reduce-scatter.39.cloned.1.call-update) | async-done | bytes 262160 | tf_op jit(solution)/shard_map/while/body/eval_jaxpr/reduce_scatter | solution.py:265
  2434.9 434.5 %while.137 = (s32[]{:T(128)}, f32[1,128,128]{2,1,0:T(8,128)S(1)}, f32[16,1,64,128]{3,2,1,0:T(8,128)}, f32[16,1,64,128]{3,2,1,0:T(8,128)}, f32[16,1,64,128]{3,2,1...) while((s32[]{:T(128)}, f32[1,128,128]{2,1,0:T(8,128)S(1)}, ...), condition=%wide.region_18.19_spmd.clone, body=%wide.region_15.18_spmd.clone.sunk | while | flops 160874752 | bytes 2876935 | solution.py:80
  2982.4 66.1 %all-reduce.17 = (f32[]{:T(128)}, f32[2048]{0:T(1024)}, f32[2048]{0:T(1024)}) all-reduce(f32[]{:T(128)} %get-tuple-element.997, f32[2048]{0:T(1024)S(1)} %copy-done.66, f32[2048]{0:T(1024)S(1)} %copy-done.63), channel_id=1, replica_groups=mesh['dp'=8,'tensor'=16] {'dp','tensor'}, use_global_device_ids=true, to_apply=%region_33.35 | all-reduce | flops 4097 | bytes 32776 | tf_op jit(solution)/shard_map/psum | solution.py:322
  3095.6 71.8 %reduce-scatter.29.cloned.1.call-done = bf16[256,1]{1,0:T(8,128)(2,1)} async-done(((bf16[2048,1]{1,0:T(8,128)(2,1)}), bf16[256,1]{1,0:T(8,128)(2,1)}) %reduce-scatter.29.cloned.1.call-update) | async-done | bytes 528
  3168.9 72.5 %reduce-scatter.21.cloned.1.call-done = bf16[128,256]{1,0:T(8,128)(2,1)} async-done(((bf16[128,2048]{1,0:T(8,128)(2,1)}), bf16[128,256]{1,0:T(8,128)(2,1)}) %reduce-scatter.21.cloned.1.call-update) | async-done | bytes 65552 | tf_op jit(solution)/shard_map/reduce_scatter | solution.py:119
  3242.9 74.6 %reduce-scatter.23.cloned.1.call-done = bf16[256,352]{0,1:T(8,128)(2,1)} async-done(((bf16[2048,352]{0,1:T(8,128)(2,1)}), bf16[256,352]{0,1:T(8,128)(2,1)}) %reduce-scatter.23.cloned.1.call-update) | async-done | bytes 180240 | tf_op jit(solution)/shard_map/reduce_scatter | solution.py:122
  3319.2 74.7 %reduce-scatter.25.cloned.1.call-done = bf16[256,352]{0,1:T(8,128)(2,1)} async-done(((bf16[2048,352]{0,1:T(8,128)(2,1)}), bf16[256,352]{0,1:T(8,128)(2,1)}) %reduce-scatter.25.cloned.1.call-update) | async-done | bytes 180240 | tf_op jit(solution)/shard_map/reduce_scatter | solution.py:125
  3395.6 74.1 %reduce-scatter.27.cloned.1.call-done = bf16[352,256]{1,0:T(8,128)(2,1)} async-done(((bf16[352,2048]{1,0:T(8,128)(2,1)}), bf16[352,256]{1,0:T(8,128)(2,1)}) %reduce-scatter.27.cloned.1.call-update) | async-done | bytes 180240 | tf_op jit(solution)/shard_map/reduce_scatter | solution.py:128
  3471.4 75.4 %reduce-scatter.19.cloned.1.call-done = bf16[256,3,128]{2,0,1:T(8,128)(2,1)} async-done(((bf16[2048,3,128]{2,0,1:T(8,128)(2,1)}), bf16[256,3,128]{2,0,1:T(8,128)(2,1)}) %reduce-scatter.19.cloned.1.call-update) | async-done | bytes 196624 | tf_op jit(solution)/shard_map/reduce_scatter | solution.py:107
  (2292 shorter events, 2259.2 us)
Async XLA Ops:
  80.0 121.5 %all-gather.8.cloned.1.call-start = ((), (), s32[]{:S(2)}) async-start(), calls=%async_computation.21 | async-start | bytes 1769472 | tf_op jit(solution)/shard_map/while/body/eval_jaxpr/all_gather | solution.py:94
  80.7 120.7 %all-gather.10.cloned.1.call-start = ((), (), s32[]{:S(2)}) async-start(), calls=%async_computation.22 | async-start | bytes 4456448 | tf_op jit(solution)/shard_map/while/body/eval_jaxpr/all_gather | solution.py:195
  84.3 486.0 %reduce-scatter.35.cloned.1.call-start = ((), (), s32[]{:S(2)}) async-start(), calls=%async_computation.23 | async-start | bytes 4456448 | tf_op jit(solution)/shard_map/while/body/eval_jaxpr/reduce_scatter | solution.py:212
  506.0 137.4 %all-gather.12.cloned.1.call-start = ((), (), s32[]{:S(2)}) async-start(), calls=%async_computation.24 | async-start | bytes 1622016 | tf_op jit(solution)/shard_map/while/body/eval_jaxpr/all_gather | solution.py:99
  579.8 121.7 %all-gather.14.cloned.1.call-start = ((), (), s32[]{:S(2)}) async-start(), calls=%async_computation.25 | async-start | bytes 1622016 | tf_op jit(solution)/shard_map/while/body/eval_jaxpr/all_gather | solution.py:100
  580.4 173.6 %all-gather.16.cloned.1.call-start = ((), (), s32[]{:S(2)}) async-start(), calls=%async_computation.26 | async-start | bytes 1622016 | tf_op jit(solution)/shard_map/while/body/eval_jaxpr/all_gather | solution.py:101
  581.0 245.5 %reduce-scatter.37.cloned.1.call-start = ((), (), s32[]{:S(2)}) async-start(), calls=%async_computation.27 | async-start | bytes 4456448 | tf_op jit(solution)/shard_map/while/body/eval_jaxpr/reduce_scatter | solution.py:232
  828.5 116.7 %reduce-scatter.39.cloned.1.call-start = ((), (), s32[]{:S(2)}) async-start(), calls=%async_computation.29 | async-start | bytes 4456448 | tf_op jit(solution)/shard_map/while/body/eval_jaxpr/reduce_scatter | solution.py:265
  949.7 566.1 %reduce-scatter.41.cloned.1.call-start = ((), (), s32[]{:S(2)}) async-start(), calls=%async_computation.31 | async-start | bytes 4456448 | tf_op jit(solution)/shard_map/while/body/eval_jaxpr/reduce_scatter | solution.py:297
  1519.3 123.8 %all-gather.8.cloned.1.call-start = ((), (), s32[]{:S(2)}) async-start(), calls=%async_computation.21 | async-start | bytes 1769472 | tf_op jit(solution)/shard_map/while/body/eval_jaxpr/all_gather | solution.py:94
  1519.9 123.2 %all-gather.10.cloned.1.call-start = ((), (), s32[]{:S(2)}) async-start(), calls=%async_computation.22 | async-start | bytes 4456448 | tf_op jit(solution)/shard_map/while/body/eval_jaxpr/all_gather | solution.py:195
  1523.5 487.2 %reduce-scatter.35.cloned.1.call-start = ((), (), s32[]{:S(2)}) async-start(), calls=%async_computation.23 | async-start | bytes 4456448 | tf_op jit(solution)/shard_map/while/body/eval_jaxpr/reduce_scatter | solution.py:212
  1947.6 135.9 %all-gather.12.cloned.1.call-start = ((), (), s32[]{:S(2)}) async-start(), calls=%async_computation.24 | async-start | bytes 1622016 | tf_op jit(solution)/shard_map/while/body/eval_jaxpr/all_gather | solution.py:99
  2020.3 121.6 %all-gather.14.cloned.1.call-start = ((), (), s32[]{:S(2)}) async-start(), calls=%async_computation.25 | async-start | bytes 1622016 | tf_op jit(solution)/shard_map/while/body/eval_jaxpr/all_gather | solution.py:100
  2020.8 173.5 %all-gather.16.cloned.1.call-start = ((), (), s32[]{:S(2)}) async-start(), calls=%async_computation.26 | async-start | bytes 1622016 | tf_op jit(solution)/shard_map/while/body/eval_jaxpr/all_gather | solution.py:101
  2021.4 245.4 %reduce-scatter.37.cloned.1.call-start = ((), (), s32[]{:S(2)}) async-start(), calls=%async_computation.27 | async-start | bytes 4456448 | tf_op jit(solution)/shard_map/while/body/eval_jaxpr/reduce_scatter | solution.py:232
  2390.0 565.9 %reduce-scatter.41.cloned.1.call-start = ((), (), s32[]{:S(2)}) async-start(), calls=%async_computation.31 | async-start | bytes 4456448 | tf_op jit(solution)/shard_map/while/body/eval_jaxpr/reduce_scatter | solution.py:297
  2964.6 129.5 %reduce-scatter.31.cloned.1.call-start = ((), (), s32[]{:S(2)}) async-start(), calls=%async_computation.19 | async-start | bytes 36864
  2967.4 200.0 %reduce-scatter.29.cloned.1.call-start = ((), (), s32[]{:S(2)}) async-start(), calls=%async_computation.18 | async-start | bytes 589824
  2969.2 272.2 %reduce-scatter.21.cloned.1.call-start = ((), (), s32[]{:S(2)}) async-start(), calls=%async_computation.14 | async-start | bytes 589824 | tf_op jit(solution)/shard_map/reduce_scatter | solution.py:119
  2970.2 347.3 %reduce-scatter.23.cloned.1.call-start = ((), (), s32[]{:S(2)}) async-start(), calls=%async_computation.15 | async-start | bytes 1622016 | tf_op jit(solution)/shard_map/reduce_scatter | solution.py:122
  2973.6 420.3 %reduce-scatter.25.cloned.1.call-start = ((), (), s32[]{:S(2)}) async-start(), calls=%async_computation.16 | async-start | bytes 1622016 | tf_op jit(solution)/shard_map/reduce_scatter | solution.py:125
  2975.1 494.6 %reduce-scatter.27.cloned.1.call-start = ((), (), s32[]{:S(2)}) async-start(), calls=%async_computation.17 | async-start | bytes 1622016 | tf_op jit(solution)/shard_map/reduce_scatter | solution.py:128
  2978.3 568.4 %reduce-scatter.19.cloned.1.call-start = ((), (), s32[]{:S(2)}) async-start(), calls=%async_computation.13 | async-start | bytes 1769472 | tf_op jit(solution)/shard_map/reduce_scatter | solution.py:107
  (168 other events, 7469.2 us)
Sparse Core Ops, SparseCore 0:
  83.4 47.3 all-gather.7
  133.2 36.7 all-gather.9
  506.1 64.1 reduce-scatter.34
  572.6 70.7 all-gather.11
  645.6 55.8 all-gather.13
  703.8 50.2 all-gather.15
  760.2 66.1 reduce-scatter.36
  828.9 35.9 all-gather.17
  877.6 67.5 reduce-scatter.38
  949.8 36.1 all-gather.19
  1448.2 67.6 reduce-scatter.40
  1522.5 49.8 all-gather.7
  1574.8 36.7 all-gather.9
  1947.8 62.9 reduce-scatter.34
  2013.0 70.5 all-gather.11
  2085.9 55.9 all-gather.13
  2144.1 50.2 all-gather.15
  2200.6 66.2 reduce-scatter.36
  2269.2 35.8 all-gather.17
  2317.8 67.5 reduce-scatter.38
  2390.1 36.0 all-gather.19
  2888.3 67.5 reduce-scatter.40
Sparse Core Ops, SparseCore 1:
  2967.4 60.9 reduce-scatter.32
  3032.6 61.4 reduce-scatter.30
  3097.5 69.9 reduce-scatter.28
  3171.4 69.9 reduce-scatter.20
  3245.2 72.3 reduce-scatter.22
  3321.7 72.1 reduce-scatter.24
  3397.5 72.1 reduce-scatter.26
  3473.8 72.9 reduce-scatter.18
